TPU v7x, 256 devices: a whole 4x4x8 slice. The times are simulated.
256 devices in a mesh: seq: 16 (over y, x), exp: 16 (over z, core).
Axes of the slice: x: 4, y: 4, z: 8, core: 2. Of those that a mesh axis runs over, the one named last changes fastest.
Arguments:
- residual: bfloat16 [16, 2048, 2048], P('exp', 'seq'), may hold values from -6 to 6
- query_nope: bfloat16 [16, 2048, 1024], P('exp', 'seq'), may hold values from -6 to 6
- query_rope: bfloat16 [16, 2048, 512], P('exp', 'seq'), may hold values from -16 to 16
- latent_rows: bfloat16 [16, 2048, 512], P('exp', 'seq'), may hold values from -6 to 6
- key_rope: bfloat16 [16, 2048, 64], P('exp', 'seq'), may hold values from -6 to 6
- key_up: bfloat16 [512, 1024], replicated, may hold values from -0.25 to 0.25
- value_up: bfloat16 [512, 1024], replicated, may hold values from -0.25 to 0.25
- output_proj: bfloat16 [1024, 2048], replicated, may hold values from -0.1875 to 0.1875
- doc_lengths: int32 [16, 8], P('exp'), may hold values from 1 to 384, 2048 in all within a row
- norm_gain: bfloat16 [2048], replicated, may hold values from 0.099609375 to 1.8984375
- router_weight: bfloat16 [2048, 64], replicated, may hold values from -0.125 to 0.125
- expert_ids: int32 [16, 2048, 6], P('exp', 'seq'), may hold values from 0 to 63, all different within a row; in each aligned block of 128 rows (0 to 127, 128 to 255, ..., all dimensions but the last counted through in order) at most 12 rows name the same one
- gate_quarter: bfloat16 [16, 16, 2048, 352], P('seq', 'exp'), may hold values from -0.125 to 0.125
- up_quarter: bfloat16 [16, 16, 2048, 352], P('seq', 'exp'), may hold values from -0.125 to 0.125
- down_quarter: bfloat16 [16, 16, 352, 2048], P('seq', 'exp'), may hold values from -0.15625 to 0.15625
Outputs:
- mixed: bfloat16 [16, 2048, 2048], P('exp', 'seq')
Inputs may be any that keep to these rules, and one draw needn't show every extreme that they name: `doc_lengths`: the longest document of each pack has exactly 384 tokens. `expert_ids`: each token names 6 different experts; the rows of one device name every expert exactly 12 times.
All inputs are finite; a program needn't handle non-finite values.
Results may differ from a plain program's by a relative error of at most 0.01.
Values may be sent and summed in bfloat16 or wider, within the bound.
A program may use at most 128 MiB of HBM per device.

v0:
```python
import math

import jax
import jax.numpy as jnp
from jax import lax
from jax.sharding import PartitionSpec as P

D = 2048
HEADS = 8
NOPE = 128
ROPE = 64
VDIM = 128
TOP = 6
KS = 3


def passed_along(block, axis, distance):
    devices = range(lax.axis_size(axis))
    route = [(i - distance, i) for i in devices if i - distance in devices]
    return lax.ppermute(block, axis, route)


def shortened(x):
    return jax.tree.map(lambda a: a.astype(jnp.bfloat16) if a.dtype == jnp.float32 else a, x)


def partner_2(value, axis, apart):
    mask = 2**apart
    pairs = [(source, source ^ mask) for source in range(lax.axis_size(axis))]
    return lax.ppermute(value, axis, pairs)


def document_of(lengths, positions):
    starts = jnp.cumsum(lengths) - lengths
    return jnp.sum((positions[:, None] >= starts[None, :]).astype(jnp.int32), axis=1) - 1


def on_device(
    residual,
    query_nope,
    query_rope,
    latent_rows,
    key_rope,
    key_up,
    value_up,
    output_proj,
    doc_lengths,
    norm_gain,
    router_weight,
    expert_ids,
    gate_quarter,
    up_quarter,
    down_quarter,
):
    row_count = residual.shape[1]
    first_row = lax.axis_index("seq") * row_count
    query_where = first_row + jnp.arange(row_count, dtype=jnp.int32)
    lengths = doc_lengths[0]
    query_docs = document_of(lengths, query_where)
    query_one = query_nope[0].reshape(row_count, HEADS, NOPE)
    query_two = query_rope[0].reshape(row_count, HEADS, ROPE)
    key_rows = jnp.dot(latent_rows[0], key_up, preferred_element_type=jnp.float32).astype(
        jnp.bfloat16
    )
    value_rows = jnp.dot(latent_rows[0], value_up, preferred_element_type=jnp.float32).astype(
        jnp.bfloat16
    )
    rope_rows = key_rope[0]
    score_scale = 1.0 / math.sqrt(NOPE + ROPE)

    def absorb(state, block_rows, begin_at):
        old_max, old_total, old_accum = state
        key_block, value_block, rope_block = block_rows
        piece_len = key_block.shape[0]
        key_where = begin_at + jnp.arange(piece_len, dtype=jnp.int32)
        key_docs = document_of(lengths, key_where)
        key_three = key_block.reshape(piece_len, HEADS, NOPE)
        value_three = value_block.reshape(piece_len, HEADS, VDIM)
        scores = jnp.einsum(
            "qhd,khd->hqk", query_one, key_three, preferred_element_type=jnp.float32
        )
        scores = (
            scores
            + jnp.einsum("qhd,kd->hqk", query_two, rope_block, preferred_element_type=jnp.float32)
        ) * score_scale
        allowed = (
            (query_docs[:, None] == key_docs[None, :])
            & (key_where[None, :] <= query_where[:, None])
            & (key_where[None, :] >= 0)
        )
        new_max = jnp.maximum(old_max, jnp.max(jnp.where(allowed[None], scores, -1e30), axis=2))
        factor = jnp.exp(old_max - new_max)
        weights = jnp.where(allowed[None], jnp.exp(scores - new_max[:, :, None]), 0.0)
        new_total = old_total * factor + jnp.sum(weights, axis=2)
        product = jnp.einsum(
            "hqk,khd->qhd",
            weights.astype(jnp.bfloat16),
            value_three,
            preferred_element_type=jnp.float32,
        )
        new_accum = old_accum * factor.T[:, :, None] + product
        return (new_max, new_total, new_accum)

    initial = (
        jnp.full((HEADS, row_count), -1e30, jnp.float32),
        jnp.zeros((HEADS, row_count), jnp.float32),
        jnp.zeros((row_count, HEADS, VDIM), jnp.float32),
    )
    state = absorb(initial, (key_rows, value_rows, rope_rows), first_row)
    for back_count in range(1, KS + 1):
        earlier = passed_along((key_rows, value_rows, rope_rows), "seq", back_count)
        state = absorb(state, earlier, first_row - back_count * row_count)
    final_max, final_total, final_accum = state
    head_out = (
        (final_accum / final_total.T[:, :, None])
        .reshape(row_count, HEADS * VDIM)
        .astype(jnp.bfloat16)
    )
    hidden_state = residual[0].astype(jnp.float32) + jnp.dot(
        head_out, output_proj, preferred_element_type=jnp.float32
    )
    normed = (
        hidden_state
        * lax.rsqrt(jnp.mean(hidden_state * hidden_state, axis=1, keepdims=True) + 1e-06)
        * norm_gain.astype(jnp.float32)
    ).astype(jnp.bfloat16)
    logits = jnp.dot(normed, router_weight, preferred_element_type=jnp.float32)
    choice_ids = expert_ids[0]
    chosen = jnp.take_along_axis(jax.nn.sigmoid(logits), choice_ids, axis=1)
    gate_values = chosen / jnp.sum(chosen, axis=1, keepdims=True) * 2.446
    seq_count = lax.axis_size("seq")
    exp_count = lax.axis_size("exp")
    experts_all = seq_count * exp_count // 4
    slot_count = row_count * TOP // experts_all // 4
    choice_flat = choice_ids.reshape(-1)
    onehot = (choice_flat[:, None] == jnp.arange(experts_all, dtype=jnp.int32)[None, :]).astype(
        jnp.int32
    )
    ranking = jnp.sum(jnp.cumsum(onehot, axis=0) * onehot, axis=1) - 1
    member = ranking % 4
    position = ranking // 4
    expert_group = choice_flat // exp_count
    column = choice_flat % exp_count
    target = ((4 * expert_group + member) * exp_count + column) * slot_count + position
    source_token = jnp.arange(row_count * TOP, dtype=jnp.int32) // TOP
    outgoing = (
        jnp.zeros((seq_count * exp_count * slot_count, D), jnp.bfloat16)
        .at[target]
        .set(normed[source_token])
    )
    arrived = lax.all_to_all(
        lax.all_to_all(
            outgoing.reshape(seq_count, exp_count, slot_count, D),
            "seq",
            split_axis=0,
            concat_axis=0,
            tiled=True,
        ),
        "exp",
        split_axis=1,
        concat_axis=1,
        tiled=True,
    )
    work_rows = arrived.reshape(-1, D)
    quarters = (gate_quarter[0, 0][None], up_quarter[0, 0][None], down_quarter[0, 0][None])
    for which_bit in range(2):
        partner = jax.tree.map(
            lambda part, own: part.astype(own.dtype),
            partner_2(shortened(quarters), "seq", which_bit),
            quarters,
        )
        quarters = tuple(
            (
                jnp.concatenate([own_part, other_part], 0)
                for own_part, other_part in zip(quarters, partner)
            )
        )
    expert_sum = jnp.zeros((work_rows.shape[0], D), jnp.float32)
    for member_index in range(4):
        activation = jax.nn.silu(
            jnp.dot(work_rows, quarters[0][member_index], preferred_element_type=jnp.float32)
        ) * jnp.dot(work_rows, quarters[1][member_index], preferred_element_type=jnp.float32)
        expert_sum = expert_sum + jnp.dot(
            activation.astype(jnp.bfloat16),
            quarters[2][member_index],
            preferred_element_type=jnp.float32,
        )
    answered = expert_sum.astype(jnp.bfloat16).reshape(seq_count, exp_count, slot_count, D)
    returned = lax.all_to_all(
        lax.all_to_all(answered, "seq", split_axis=0, concat_axis=0, tiled=True),
        "exp",
        split_axis=1,
        concat_axis=1,
        tiled=True,
    )
    back_rows = returned.reshape(-1, D)[target]
    weighted = back_rows.astype(jnp.float32) * gate_values.reshape(-1)[:, None]
    routed = jnp.sum(weighted.reshape(row_count, TOP, D), axis=1)
    return (hidden_state + routed).astype(jnp.bfloat16)[None]


def solution(mesh):
    in_specs = (
        P("exp", "seq", None),
        P("exp", "seq", None),
        P("exp", "seq", None),
        P("exp", "seq", None),
        P("exp", "seq", None),
        P(),
        P(),
        P(),
        P("exp", None),
        P(),
        P(),
        P("exp", "seq", None),
        P("seq", "exp", None, None),
        P("seq", "exp", None, None),
        P("seq", "exp", None, None),
    )
    out_specs = P("exp", "seq", None)
    return jax.shard_map(
        on_device, mesh=mesh, in_specs=in_specs, out_specs=out_specs, check_vma=False
    )
```

profile of v0, /device:TPU:8, one launch (start us, length us, event | category | flops | bytes accessed | tf_op | source)
XLA Modules:
  0.0 645.1 jit_solution(15897547125463165674)
XLA Ops:
  0.0 5.1 collective-permute-start.4
  5.1 2.5 collective-permute-start.1
  7.6 5.6 collective-permute-start.7
  14.4 2.6 collective-permute-start.8
  17.0 3.4 collective-permute-start.5
  31.6 2.5 collective-permute-start.2
  34.4 3.1 collective-permute-start.6
  38.4 2.2 collective-permute-start.3
  41.5 11.1 %collective-permute-done.6 = bf16[128,1024]{1,0:T(8,128)(2,1)S(1)} collective-permute-done((bf16[128,1024]{1,0:T(8,128)(2,1)}, bf16[128,1024]{1,0:T(8,128)(2,1)S(1)}, u32[]{:S(2)}, u32[]{:S(2)}) %collective-permute-start.6) | collective-permute-done | bytes 262176 | tf_op jit(solution)/shard_map/ppermute | solution.py:20
  55.2 8.0 %collective-permute-done = bf16[128,1024]{1,0:T(8,128)(2,1)S(1)} collective-permute-done((bf16[128,1024]{1,0:T(8,128)(2,1)}, bf16[128,1024]{1,0:T(8,128)(2,1)S(1)}, u32[]{:S(2)}, u32[]{:S(2)}) %collective-permute-start) | collective-permute-done | bytes 262176 | tf_op jit(solution)/shard_map/ppermute | solution.py:20
  73.8 3.0 multiply_reduce_fusion.1
  78.7 29.0 %scatter_custom_fusion = bf16[768,2048]{1,0:T(8,128)(2,1)S(1)} fusion(s32[768]{0:T(1024)S(1)} %copy-done.24, bf16[128,2048]{1,0:T(8,128)(2,1)} %multiply_convert_fusion.3, s32[1024]{0:T(1024)} %pad_clamp_fusion.1, bf16[]{:T(256)} %constant.121.clone.1), kind=kCustom, calls=%fused_computation.6 | custom fusion | bytes 3146240 | tf_op jit(solution)/shard_map/scatter | solution.py:149
  107.8 4.9 reshape.762
  112.6 4.7 copy.110
  117.3 35.4 %all_to_all.20 = bf16[16,16,3,2048]{3,1,2,0:T(8,128)(2,1)S(1)} all-to-all(bf16[16,16,3,2048]{3,1,2,0:T(8,128)(2,1)S(1)} %copy.110), channel_id=1, replica_groups=mesh['seq'=16,'exp'=16] {'seq'}, dimensions={0} | all-to-all | bytes 6291456 | tf_op jit(solution)/shard_map/all_to_all | solution.py:152
  152.8 3.4 copy.111
  156.2 8.6 %all-to-all-start.1 = ((bf16[16,16,3,2048]{3,0,2,1:T(8,128)(2,1)}), bf16[16,16,3,2048]{3,0,2,1:T(8,128)(2,1)S(1)}, u32[]{:S(2)}, u32[]{:S(2)}) async-start(bf16[16,16,3,2048]{3,0,2,1:T(8,128)(2,1)} %copy.111), calls=%async_computation.1 | async-start | bytes 6291456 | tf_op jit(solution)/shard_map/all_to_all | solution.py:151
  165.2 33.8 %collective-permute-done.10 = bf16[1,2048,352]{1,2,0:T(8,128)(2,1)S(1)} collective-permute-done((bf16[1,2048,352]{1,2,0:T(8,128)(2,1)}, bf16[1,2048,352]{1,2,0:T(8,128)(2,1)S(1)}, u32[]{:S(2)}, u32[]{:S(2)}) %collective-permute-start.10) | collective-permute-done | bytes 1441824 | tf_op jit(solution)/shard_map/ppermute | solution.py:30
  199.0 3.7 pad_maximum_fusion.1
  206.4 93.0 %collective-permute-done.9 = bf16[1,2048,352]{1,2,0:T(8,128)(2,1)S(1)} collective-permute-done((bf16[1,2048,352]{1,2,0:T(8,128)(2,1)S(1)}, bf16[1,2048,352]{1,2,0:T(8,128)(2,1)S(1)}, u32[]{:S(2)}, u32[]{:S(2)}) %collective-permute-start.9) | collective-permute-done | bytes 1441824 | tf_op jit(solution)/shard_map/ppermute | solution.py:30
  299.4 2.0 pad_maximum_fusion
  301.5 2.3 collective-permute-start.12
  303.7 26.6 %collective-permute-done.11 = bf16[1,352,2048]{2,1,0:T(8,128)(2,1)S(1)} collective-permute-done((bf16[1,352,2048]{2,1,0:T(8,128)(2,1)S(1)}, bf16[1,352,2048]{2,1,0:T(8,128)(2,1)S(1)}, u32[]{:S(2)}, u32[]{:S(2)}) %collective-permute-start.11) | collective-permute-done | bytes 1441824 | tf_op jit(solution)/shard_map/ppermute | solution.py:30
  332.3 2.3 collective-permute-start.14
  334.6 4.7 copy.112
  339.3 7.7 %reshape.763 = bf16[768,2048]{1,0:T(8,128)(2,1)S(1)} reshape(bf16[16,16,3,2048]{3,2,1,0:T(4,128)(2,1)} %copy.112) | data formatting | bytes 6291456 | tf_op jit(solution)/shard_map/reshape | solution.py:164
  347.0 3.9 fusion.19
  350.9 2.3 fusion.11
  353.2 3.7 fusion.4
  356.9 3.7 fusion.7
  360.5 8.5 %fusion.15 = f32[768,2048]{1,0:T(8,128)} fusion(bf16[1,1,352,2048]{3,2,1,0:T(8,128)(2,1)} %param.29, bf16[768,2048]{1,0:T(8,128)(2,1)S(1)} %reshape.763, bf16[1,1,2048,352]{2,3,1,0:T(8,128)(2,1)} %param.28, f32[768,352]{0,1:T(8,128)} %fusion.19), kind=kOutput, calls=%fused_computation.31 | convolution fusion | flops 2216214528 | bytes 13402112 | tf_op jit(solution)/shard_map/dot_general | solution.py:183
  369.1 8.6 %fusion.9 = f32[768,2048]{1,0:T(8,128)} fusion(bf16[1,352,2048]{2,1,0:T(8,128)(2,1)} %copy-done.9, f32[768,352]{0,1:T(8,128)} %fusion.11, bf16[768,2048]{1,0:T(8,128)(2,1)S(1)} %reshape.763, bf16[1,2048,352]{1,2,0:T(8,128)(2,1)} %copy-done.8), kind=kOutput, calls=%fused_computation.25 | convolution fusion | flops 2216214528 | bytes 13402112 | tf_op jit(solution)/shard_map/dot_general | solution.py:183
  377.6 15.9 %collective-permute-done.12 = bf16[2,2048,352]{1,2,0:T(8,128)(2,1)} collective-permute-done((bf16[2,2048,352]{1,2,0:T(8,128)(2,1)}, bf16[2,2048,352]{1,2,0:T(8,128)(2,1)}, u32[]{:S(2)}, u32[]{:S(2)}) %collective-permute-start.12) | collective-permute-done | bytes 2883616 | tf_op jit(solution)/shard_map/ppermute | solution.py:30
  393.5 60.4 %collective-permute-done.14 = bf16[2,352,2048]{2,1,0:T(8,128)(2,1)} collective-permute-done((bf16[2,352,2048]{2,1,0:T(8,128)(2,1)}, bf16[2,352,2048]{2,1,0:T(8,128)(2,1)}, u32[]{:S(2)}, u32[]{:S(2)}) %collective-permute-start.14) | collective-permute-done | bytes 2883616 | tf_op jit(solution)/shard_map/ppermute | solution.py:30
  454.0 8.7 %fusion.6 = f32[768,2048]{1,0:T(8,128)} fusion(bf16[2,352,2048]{2,1,0:T(8,128)(2,1)} %collective-permute-done.14, f32[768,352]{0,1:T(8,128)} %fusion.7, bf16[768,2048]{1,0:T(8,128)(2,1)S(1)} %reshape.763, bf16[2,2048,352]{1,2,0:T(8,128)(2,1)} %collective-permute-done.12), kind=kOutput, calls=%fused_computation.20 | convolution fusion | flops 2216214528 | bytes 13402112 | tf_op jit(solution)/shard_map/dot_general | solution.py:183
  462.7 13.3 %add_convert_fusion = bf16[768,2048]{1,0:T(8,128)(2,1)} fusion(f32[768,2048]{1,0:T(8,128)} %fusion.6, f32[768,2048]{1,0:T(8,128)} %fusion.15, f32[768,2048]{1,0:T(8,128)} %fusion.9, bf16[2,352,2048]{2,1,0:T(8,128)(2,1)} %collective-permute-done.14, f32[768,352]{0,1:T(8,128)} %fusion.4, bf16[768,2048]{1,0:T(8,128)(2,1)S(1)} %reshape.763, ...), kind=kOutput, calls=%fused_computation.5 | convolution fusion | flops 2222505984 | bytes 29130752 | tf_op jit(solution)/shard_map/dot_general | solution.py:183
  476.0 9.1 %reshape.764 = bf16[16,16,3,2048]{3,2,1,0:T(4,128)(2,1)} reshape(bf16[768,2048]{1,0:T(8,128)(2,1)} %add_convert_fusion) | data formatting | bytes 6291456 | tf_op jit(solution)/shard_map/reshape | solution.py:188
  485.1 4.7 copy.113
  489.8 41.6 %all_to_all.21 = bf16[16,16,3,2048]{3,1,2,0:T(8,128)(2,1)S(1)} all-to-all(bf16[16,16,3,2048]{3,1,2,0:T(8,128)(2,1)S(1)} %copy.113), channel_id=1, replica_groups=mesh['seq'=16,'exp'=16] {'seq'}, dimensions={0} | all-to-all | bytes 6291456 | tf_op jit(solution)/shard_map/all_to_all | solution.py:190
  531.4 3.3 copy.114
  534.7 7.4 %all-to-all-start.3 = ((bf16[16,16,3,2048]{3,0,2,1:T(8,128)(2,1)}), bf16[16,16,3,2048]{3,0,2,1:T(8,128)(2,1)S(1)}, u32[]{:S(2)}, u32[]{:S(2)}) async-start(bf16[16,16,3,2048]{3,0,2,1:T(8,128)(2,1)} %copy.114), calls=%async_computation.3 | async-start | bytes 6291456 | tf_op jit(solution)/shard_map/all_to_all | solution.py:189
  545.3 5.1 gather_fusion.1
  550.8 63.1 %all-to-all-done.3 = bf16[16,16,3,2048]{3,0,2,1:T(8,128)(2,1)S(1)} async-done(((bf16[16,16,3,2048]{3,0,2,1:T(8,128)(2,1)}), bf16[16,16,3,2048]{3,0,2,1:T(8,128)(2,1)S(1)}, u32[]{:S(2)}, u32[]{:S(2)}) %all-to-all-start.3) | async-done | bytes 3145760 | tf_op jit(solution)/shard_map/all_to_all | solution.py:189
  613.9 4.7 copy.115
  618.6 7.5 %reshape.765 = bf16[768,2048]{1,0:T(8,128)(2,1)S(1)} reshape(bf16[16,16,3,2048]{3,2,1,0:T(4,128)(2,1)} %copy.115) | data formatting | bytes 6291456 | tf_op jit(solution)/shard_map/reshape | solution.py:196
  626.1 4.2 gather_fusion
  630.3 6.6 %reshape.767 = f32[128,6,2048]{2,1,0:T(8,128)} reshape(bf16[768,2048]{1,0:T(8,128)(2,1)} %gather_fusion) | data formatting | bytes 9437184 | tf_op jit(solution)/shard_map/convert_element_type | solution.py:197
  636.9 6.8 %multiply_reduce_fusion = f32[128,2048]{1,0:T(8,128)S(1)} fusion(f32[128,6,2048]{2,1,0:T(8,128)} %reshape.767, f32[128,6]{1,0:T(8,128)S(1)} %divide_multiply_fusion), kind=kLoop, calls=%fused_computation.4 | loop fusion | flops 2883584 | bytes 7343104 | tf_op jit(solution)/shard_map/reduce_sum | solution.py:198
  (134 shorter events, 39.7 us)
Async XLA Ops:
  0.0 13.2 %copy-start = (bf16[512,1024]{1,0:T(8,128)(2,1)S(1)}, bf16[512,1024]{1,0:T(8,128)(2,1)}, u32[]{:S(2)}) copy-start(bf16[512,1024]{1,0:T(8,128)(2,1)} %param.21) | copy-start | bytes 3145732
  0.0 26.6 %copy-start.14 = (bf16[1,128,512]{2,1,0:T(8,128)(2,1)S(1)}, bf16[1,128,512]{2,1,0:T(8,128)(2,1)}, u32[]{:S(2)}) copy-start(bf16[1,128,512]{2,1,0:T(8,128)(2,1)} %param.18) | copy-start | bytes 393220
  0.0 26.6 %copy-start.10 = (bf16[512,1024]{1,0:T(8,128)(2,1)S(1)}, bf16[512,1024]{1,0:T(8,128)(2,1)}, u32[]{:S(2)}) copy-start(bf16[512,1024]{1,0:T(8,128)(2,1)} %param.20) | copy-start | bytes 3145732
  0.0 27.6 %copy-start.16 = (bf16[1,128,1024]{2,1,0:T(8,128)(2,1)S(1)}, bf16[1,128,1024]{2,1,0:T(8,128)(2,1)}, u32[]{:S(2)}) copy-start(bf16[1,128,1024]{2,1,0:T(8,128)(2,1)} %param.16) | copy-start | bytes 786436
  0.0 29.9 %copy-start.20 = (bf16[1,128,64]{1,2,0:T(8,128)(2,1)S(1)}, bf16[1,128,64]{1,2,0:T(8,128)(2,1)}, u32[]{:S(2)}) copy-start(bf16[1,128,64]{1,2,0:T(8,128)(2,1)} %param.19) | copy-start | bytes 49156
  0.0 34.3 %collective-permute-start.4 = (bf16[128,64]{0,1:T(8,128)(2,1)}, bf16[128,64]{0,1:T(8,128)(2,1)S(1)}, u32[]{:S(2)}, u32[]{:S(2)}) collective-permute-start(bf16[128,64]{0,1:T(8,128)(2,1)} %bitcast.323), channel_id=1, source_target_pairs={{0,32},{16,48},{32,64},{48,80},{64,96},{80,112},{96,128},{112,144}... | collective-permute-start | bytes 49160 | tf_op jit(solution)/shard_map/ppermute | solution.py:20
  5.1 32.6 %collective-permute-start.1 = (bf16[128,64]{0,1:T(8,128)(2,1)}, bf16[128,64]{0,1:T(8,128)(2,1)S(1)}, u32[]{:S(2)}, u32[]{:S(2)}) collective-permute-start(bf16[128,64]{0,1:T(8,128)(2,1)} %bitcast.324), channel_id=1, source_target_pairs={{0,16},{16,32},{32,48},{48,64},{64,80},{80,96},{96,112},{112,128},... | collective-permute-start | bytes 49160 | tf_op jit(solution)/shard_map/ppermute | solution.py:20
  7.6 24.0 %collective-permute-start.7 = (bf16[128,64]{0,1:T(8,128)(2,1)}, bf16[128,64]{0,1:T(8,128)(2,1)S(1)}, u32[]{:S(2)}, u32[]{:S(2)}) collective-permute-start(bf16[128,64]{0,1:T(8,128)(2,1)} %bitcast.325), channel_id=1, source_target_pairs={{0,48},{16,64},{32,80},{48,96},{64,112},{80,128},{96,144},{112,160... | collective-permute-start | bytes 49160 | tf_op jit(solution)/shard_map/ppermute | solution.py:20
  14.4 50.5 %collective-permute-start.8 = (bf16[128,1024]{1,0:T(8,128)(2,1)S(1)}, bf16[128,1024]{1,0:T(8,128)(2,1)}, u32[]{:S(2)}, u32[]{:S(2)}) collective-permute-start(bf16[128,1024]{1,0:T(8,128)(2,1)S(1)} %convolution_convert_fusion), channel_id=1, source_target_pairs={{0,48},{16,64},{32,80},{48,96},{64,112},{80,128},{96,144},{112,160... | collective-permute-start | bytes 786440 | tf_op jit(solution)/shard_map/ppermute | solution.py:20
  17.0 50.1 %collective-permute-start.5 = (bf16[128,1024]{1,0:T(8,128)(2,1)S(1)}, bf16[128,1024]{1,0:T(8,128)(2,1)}, u32[]{:S(2)}, u32[]{:S(2)}) collective-permute-start(bf16[128,1024]{1,0:T(8,128)(2,1)S(1)} %convolution_convert_fusion), channel_id=1, source_target_pairs={{0,32},{16,48},{32,64},{48,80},{64,96},{80,112},{96,128},{112,144}... | collective-permute-start | bytes 786440 | tf_op jit(solution)/shard_map/ppermute | solution.py:20
  24.3 6.7 %copy-start.27 = (bf16[2048]{0:T(1024)(128)(2,1)S(1)}, bf16[2048]{0:T(1024)(128)(2,1)}, u32[]{:S(2)}) copy-start(bf16[2048]{0:T(1024)(128)(2,1)} %param.24) | copy-start | bytes 12292
  31.6 39.6 %collective-permute-start.2 = (bf16[128,1024]{1,0:T(8,128)(2,1)S(1)}, bf16[128,1024]{1,0:T(8,128)(2,1)}, u32[]{:S(2)}, u32[]{:S(2)}) collective-permute-start(bf16[128,1024]{1,0:T(8,128)(2,1)S(1)} %convolution_convert_fusion), channel_id=1, source_target_pairs={{0,16},{16,32},{32,48},{48,64},{64,80},{80,96},{96,112},{112,128},... | collective-permute-start | bytes 786440 | tf_op jit(solution)/shard_map/ppermute | solution.py:20
  34.4 18.2 %collective-permute-start.6 = (bf16[128,1024]{1,0:T(8,128)(2,1)}, bf16[128,1024]{1,0:T(8,128)(2,1)S(1)}, u32[]{:S(2)}, u32[]{:S(2)}) collective-permute-start(bf16[128,1024]{1,0:T(8,128)(2,1)} %convolution_convert_fusion.1), channel_id=1, source_target_pairs={{0,48},{16,64},{32,80},{48,96},{64,112},{80,128},{96,144},{112,160... | collective-permute-start | bytes 786440 | tf_op jit(solution)/shard_map/ppermute | solution.py:20
  37.8 0.6 copy-start.25
  38.4 16.5 %collective-permute-start.3 = (bf16[128,1024]{1,0:T(8,128)(2,1)}, bf16[128,1024]{1,0:T(8,128)(2,1)S(1)}, u32[]{:S(2)}, u32[]{:S(2)}) collective-permute-start(bf16[128,1024]{1,0:T(8,128)(2,1)} %convolution_convert_fusion.1), channel_id=1, source_target_pairs={{0,32},{16,48},{32,64},{48,80},{64,96},{80,112},{96,128},{112,144}... | collective-permute-start | bytes 786440 | tf_op jit(solution)/shard_map/ppermute | solution.py:20
  52.6 10.6 %collective-permute-start = (bf16[128,1024]{1,0:T(8,128)(2,1)}, bf16[128,1024]{1,0:T(8,128)(2,1)S(1)}, u32[]{:S(2)}, u32[]{:S(2)}) collective-permute-start(bf16[128,1024]{1,0:T(8,128)(2,1)} %convolution_convert_fusion.1), channel_id=1, source_target_pairs={{0,16},{16,32},{32,48},{48,64},{64,80},{80,96},{96,112},{112,128},... | collective-permute-start | bytes 786440 | tf_op jit(solution)/shard_map/ppermute | solution.py:20
  63.5 1.4 copy-start.17
  63.5 5.8 copy-start.21
  67.1 2.5 copy-start.18
  67.1 2.5 copy-start.22
  67.1 2.5 copy-start.23
  67.1 5.3 copy-start.12
  69.3 3.1 copy-start.13
  69.4 4.3 copy-start.11
  73.7 4.0 copy-start.19
  73.7 5.0 copy-start.24
  76.8 1.0 copy-start.2
  156.2 178.4 %all-to-all-start.1 = ((bf16[16,16,3,2048]{3,0,2,1:T(8,128)(2,1)}), bf16[16,16,3,2048]{3,0,2,1:T(8,128)(2,1)S(1)}, u32[]{:S(2)}, u32[]{:S(2)}) async-start(bf16[16,16,3,2048]{3,0,2,1:T(8,128)(2,1)} %copy.111), calls=%async_computation.1 | async-start | bytes 6291456 | tf_op jit(solution)/shard_map/all_to_all | solution.py:151
  164.8 39.6 %copy-start.4 = (bf16[1,1,2048,352]{2,3,1,0:T(8,128)(2,1)S(1)}, bf16[1,1,2048,352]{2,3,1,0:T(8,128)(2,1)}, u32[]{:S(2)}) copy-start(bf16[1,1,2048,352]{2,3,1,0:T(8,128)(2,1)} %param.27) | copy-start | bytes 4325380
  164.8 40.1 %copy-start.5 = (bf16[1,1,352,2048]{3,2,1,0:T(8,128)(2,1)S(1)}, bf16[1,1,352,2048]{3,2,1,0:T(8,128)(2,1)}, u32[]{:S(2)}) copy-start(bf16[1,1,352,2048]{3,2,1,0:T(8,128)(2,1)} %param.29) | copy-start | bytes 4325380
  164.8 34.2 %collective-permute-start.10 = (bf16[1,2048,352]{1,2,0:T(8,128)(2,1)}, bf16[1,2048,352]{1,2,0:T(8,128)(2,1)S(1)}, u32[]{:S(2)}, u32[]{:S(2)}) collective-permute-start(bf16[1,2048,352]{1,2,0:T(8,128)(2,1)} %bitcast.315), channel_id=1, source_target_pairs={{0,16},{16,0},{32,48},{48,32},{64,80},{80,64},{96,112},{112,96},{1... | collective-permute-start | bytes 4325384 | tf_op jit(solution)/shard_map/ppermute | solution.py:30
  199.0 3.7 copy-start.6
  202.7 150.5 %collective-permute-start.13 = (bf16[2,2048,352]{1,2,0:T(8,128)(2,1)}, bf16[2,2048,352]{1,2,0:T(8,128)(2,1)}, u32[]{:S(2)}, u32[]{:S(2)}) collective-permute-start(bf16[2,2048,352]{1,2,0:T(8,128)(2,1)} %pad_maximum_fusion.1), channel_id=1, source_target_pairs={{0,32},{16,48},{32,0},{48,16},{64,96},{80,112},{96,64},{112,80},{1... | collective-permute-start | bytes 8650760 | tf_op jit(solution)/shard_map/ppermute | solution.py:30
  204.4 95.0 %collective-permute-start.9 = (bf16[1,2048,352]{1,2,0:T(8,128)(2,1)S(1)}, bf16[1,2048,352]{1,2,0:T(8,128)(2,1)S(1)}, u32[]{:S(2)}, u32[]{:S(2)}) collective-permute-start(bf16[1,2048,352]{1,2,0:T(8,128)(2,1)S(1)} %bitcast.311), channel_id=1, source_target_pairs={{0,16},{16,0},{32,48},{48,32},{64,80},{80,64},{96,112},{112,96},{1... | collective-permute-start | bytes 4325384 | tf_op jit(solution)/shard_map/ppermute | solution.py:30
  204.9 125.4 %collective-permute-start.11 = (bf16[1,352,2048]{2,1,0:T(8,128)(2,1)S(1)}, bf16[1,352,2048]{2,1,0:T(8,128)(2,1)S(1)}, u32[]{:S(2)}, u32[]{:S(2)}) collective-permute-start(bf16[1,352,2048]{2,1,0:T(8,128)(2,1)S(1)} %bitcast.313), channel_id=1, source_target_pairs={{0,16},{16,0},{32,48},{48,32},{64,80},{80,64},{96,112},{112,96},{1... | collective-permute-start | bytes 4325384 | tf_op jit(solution)/shard_map/ppermute | solution.py:30
  299.4 2.1 copy-start.8
  301.5 92.1 %collective-permute-start.12 = (bf16[2,2048,352]{1,2,0:T(8,128)(2,1)}, bf16[2,2048,352]{1,2,0:T(8,128)(2,1)}, u32[]{:S(2)}, u32[]{:S(2)}) collective-permute-start(bf16[2,2048,352]{1,2,0:T(8,128)(2,1)} %pad_maximum_fusion), channel_id=1, source_target_pairs={{0,32},{16,48},{32,0},{48,16},{64,96},{80,112},{96,64},{112,80},{1... | collective-permute-start | bytes 8650760 | tf_op jit(solution)/shard_map/ppermute | solution.py:30
  330.3 2.0 copy-start.9
  332.3 121.6 %collective-permute-start.14 = (bf16[2,352,2048]{2,1,0:T(8,128)(2,1)}, bf16[2,352,2048]{2,1,0:T(8,128)(2,1)}, u32[]{:S(2)}, u32[]{:S(2)}) collective-permute-start(bf16[2,352,2048]{2,1,0:T(8,128)(2,1)} %pad_maximum_fusion.2), channel_id=1, source_target_pairs={{0,32},{16,48},{32,0},{48,16},{64,96},{80,112},{96,64},{112,80},{1... | collective-permute-start | bytes 8650760 | tf_op jit(solution)/shard_map/ppermute | solution.py:30
  347.0 3.9 copy-start.7
  534.7 7.4 %copy-start.26 = (s32[1,128,6]{1,0,2:T(1,128)S(1)}, s32[1,128,6]{1,0,2:T(1,128)}, u32[]{:S(2)}) copy-start(s32[1,128,6]{1,0,2:T(1,128)} %param.26) | copy-start | bytes 9220
  534.7 9.2 %copy-start.15 = (bf16[2048,64]{0,1:T(8,128)(2,1)S(1)}, bf16[2048,64]{0,1:T(8,128)(2,1)}, u32[]{:S(2)}) copy-start(bf16[2048,64]{0,1:T(8,128)(2,1)} %param.25) | copy-start | bytes 786436
  534.7 79.2 %all-to-all-start.3 = ((bf16[16,16,3,2048]{3,0,2,1:T(8,128)(2,1)}), bf16[16,16,3,2048]{3,0,2,1:T(8,128)(2,1)S(1)}, u32[]{:S(2)}, u32[]{:S(2)}) async-start(bf16[16,16,3,2048]{3,0,2,1:T(8,128)(2,1)} %copy.114), calls=%async_computation.3 | async-start | bytes 6291456 | tf_op jit(solution)/shard_map/all_to_all | solution.py:189
  636.9 6.8 %copy-start.3 = (f32[128,2048]{1,0:T(8,128)S(1)}, f32[128,2048]{1,0:T(8,128)}, u32[]{:S(2)}) copy-start(f32[128,2048]{1,0:T(8,128)} %copy-done.2) | copy-start | bytes 3145732
  636.9 7.7 %copy-start.1 = (bf16[512,1024]{1,0:T(8,128)(2,1)S(1)}, bf16[512,1024]{1,0:T(8,128)(2,1)}, u32[]{:S(2)}) copy-start(bf16[512,1024]{1,0:T(8,128)(2,1)} %param.21) | copy-start | bytes 3145732
where the time goes:
time: 655 us; the launch traced here: 645 us
  waiting for transfers between devices  312 us (48%)
  local copies, waits for them, and re-layouts  109 us (17%)
  blocking collectives  77 us (12%)
  matrix products  67.6 us (10%)
  starting transfers between devices  53.5 us (8%)
  other arithmetic  24.5 us (4%)
    ppermute x6, waiting for transfers between devices, partner_2(): return lax.ppermute(value, axis, pairs)  230 us
    all_to_all x1, waiting for transfers between devices, on_device(): lax.all_to_all(lax.all_to_all(answered, 'seq', split_axis=0, concat_axis=...  63.1 us
    all_to_all x1, blocking collectives, on_device(): lax.all_to_all(answered, 'seq', split_axis=0, concat_axis=0, tiled=True)  41.6 us
    dot_general x4, matrix products, on_device(): jnp.dot(activation.astype(jnp.bfloat16), quarters[2][member_index], prefe...  39.1 us
    all_to_all x1, blocking collectives, on_device(): lax.all_to_all(outgoing.reshape(seq_count, exp_count, slot_count, D), 'se...  35.4 us
    scatter x1, local copies, waits for them, and re-layouts, on_device(): outgoing = jnp.zeros((seq_count * exp_count * slot_count, D), jnp.bfloat1...  29 us
    ppermute x9, starting transfers between devices, passed_along(): return lax.ppermute(block, axis, route)  28.8 us
    ppermute x9, waiting for transfers between devices, passed_along(): return lax.ppermute(block, axis, route)  19.1 us
  transfers between devices with their start and end apart: 17, of which 8 were waited for; matrix products, arithmetic and copies ran while one was open for 13% of the time, Pallas kernels for 0%

commit v1 on v0

v1 whole, which is shorter than its diff:
```python
import functools
import math

import jax
import jax.numpy as jnp
from jax import lax
from jax.experimental import pallas as pl
from jax.experimental.pallas import tpu as pltpu
from jax.sharding import PartitionSpec as P

MESH = pl.DeviceIdType.MESH
F32 = jnp.float32
BF16 = jnp.bfloat16

D = 2048
HEADS = 8
NOPE = 128
ROPE = 64
LATENT = 512
TOP = 6
KS = 3
T = 128
EXPERTS = 64
FQ = 352
SLOTS = 12
NX, NY, NZ = 4, 4, 8
BLOCK = NZ * SLOTS
WORK = 2 * NY * BLOCK
EXTRA = 128
NC = 4
CW = D // NC
NJ = 4
JW = D // NJ


def dot(a, b):
    return jnp.dot(a, b, preferred_element_type=F32)


def dot_t(a, b):
    return lax.dot_general(a, b, (((1,), (1,)), ((), ())), preferred_element_type=F32)


def iota(shape, dim):
    return lax.broadcasted_iota(jnp.int32, shape, dim).astype(F32)


def lanes_of(c):
    if c == 0:
        return pl.ds(0, EXTRA + CW)
    return pl.ds(EXTRA + c * CW, CW)


def kernel(
    residual,
    query_nope,
    query_rope,
    latent,
    rope,
    lengths,
    gain,
    router,
    ids,
    key_up_in,
    value_up_in,
    proj_in,
    gate_in,
    up_in,
    down_in,
    out,
    key_up,
    value_up,
    proj,
    w_gate,
    w_up,
    w_down,
    latents,
    keys,
    values,
    head_out,
    hidden,
    tok,
    code_rows,
    code_cols,
    pick,
    put,
    outbox,
    work,
    units,
    inbox,
    zs,
    zr,
    load_sem,
    a_send,
    a_recv,
    w_send,
    w_recv,
    f_send,
    f_recv,
    d_send,
    d_recv,
    e_send,
    e_recv,
    z_send,
    z_recv,
    y_send,
    y_recv,
    r_send,
    r_recv,
    s_send,
    s_recv,
):
    seq = lax.axis_index("seq")
    exp = lax.axis_index("exp")
    my_y, my_x = lax.div(seq, NX), lax.rem(seq, NX)
    my_z, my_c = lax.div(exp, 2), lax.rem(exp, 2)

    def peer(dx=0, dy=0, dz=0, dc=0):
        x = lax.rem(my_x + (dx + NX), NX)
        y = lax.rem(my_y + (dy + NY), NY)
        z = lax.rem(my_z + (dz + NZ), NZ)
        c = lax.rem(my_c + dc, 2)
        return (y * NX + x, z * 2 + c)

    def later(distance):
        return (lax.rem(seq + (distance + NX * NY), NX * NY), exp)

    def send(src, dst, send_sem, recv_sem, device):
        copy = pltpu.make_async_remote_copy(
            src_ref=src,
            dst_ref=dst,
            send_sem=send_sem,
            recv_sem=recv_sem,
            device_id=device,
            device_id_type=MESH,
        )
        copy.start()
        return copy

    started = []

    loads = []
    for i, (src, dst) in enumerate(
        (
            (key_up_in, key_up),
            (value_up_in, value_up),
            (proj_in, proj),
            (gate_in.at[0, 0], w_gate.at[0]),
            (up_in.at[0, 0], w_up.at[0]),
            (down_in.at[0, 0], w_down.at[0]),
        )
    ):
        copy = pltpu.make_async_copy(src, dst, load_sem.at[i])
        copy.start()
        loads.append(copy)

    partners = [later(d) for d in (1, 2, 3, -1, -2, -3)]
    partners += [peer(dx=1), peer(dx=-1), peer(dz=1), peer(dz=-1)]
    partners += [peer(dy=b // 2, dc=b % 2) for b in range(1, 2 * NY)]
    barrier = pltpu.get_barrier_semaphore()
    for device in partners:
        pl.semaphore_signal(barrier, inc=1, device_id=device, device_id_type=MESH)

    twice = (
        lax.rem(lax.broadcasted_iota(jnp.int32, (ROPE, 2 * ROPE), 1), ROPE)
        == lax.broadcasted_iota(jnp.int32, (ROPE, 2 * ROPE), 0)
    ).astype(F32).astype(BF16)
    latents[0, :, :LATENT] = latent[0]
    latents[0, :, LATENT:] = dot(rope[0], twice).astype(BF16)

    pl.semaphore_wait(barrier, len(partners))

    arriving = []
    for d in (1, 2, 3):
        copy = send(latents.at[0], latents.at[d], a_send.at[d - 1], a_recv.at[d - 1], later(d))
        arriving.append(copy)
        started.append(copy)

    near = []
    for i, (src, dst) in enumerate(((gate_in, w_gate), (up_in, w_up))):
        for way, dx in ((0, 1), (1, -1)):
            copy = send(
                src.at[0, 0], dst.at[1 + way], w_send.at[i, way], w_recv.at[i, way], peer(dx=dx)
            )
            near.append(copy)
            started.append(copy)

    lane_e = iota((T, EXPERTS), 1)
    id_cols = ids[0].astype(F32)
    hits = [(id_cols[:, j : j + 1] == lane_e).astype(F32) for j in range(TOP)]
    named = functools.reduce(jnp.add, hits)
    lower = (
        lax.broadcasted_iota(jnp.int32, (T, T), 0) >= lax.broadcasted_iota(jnp.int32, (T, T), 1)
    ).astype(F32).astype(BF16)
    counted = dot(lower, named.astype(BF16))
    ranks = [jnp.sum(hit * counted, axis=1, keepdims=True) - 1.0 for hit in hits]

    def codes(shape, dim):
        row = iota(shape, dim)
        block = jnp.floor((row + 0.5) * (1.0 / BLOCK))
        rest = row - block * BLOCK
        source = jnp.floor((rest + 0.5) * (1.0 / SLOTS))
        rank = rest - source * SLOTS
        dy = jnp.floor((block + 0.5) * 0.5)
        dc = block - dy * 2.0
        y = dy + my_y.astype(F32)
        y = jnp.where(y >= NY, y - NY, y)
        c = dc + my_c.astype(F32)
        c = jnp.where(c >= 2.0, c - 2.0, c)
        expert = y * 16.0 + my_z.astype(F32) * 2.0 + c
        return source * 1024.0 + expert * 16.0 + rank

    code_rows[...] = codes((WORK, T), 0)
    code_cols[...] = codes((8, WORK), 1)

    loads[0].wait()
    loads[1].wait()

    def project(d):
        rows = pl.ds(pl.multiple_of(d * T, T), T)
        block = latents[d, :, :LATENT]
        keys[rows, :] = dot(block, key_up[...]).astype(BF16)
        values[rows, :] = dot(block, value_up[...]).astype(BF16)

    project(0)
    for copy in arriving:
        copy.wait_recv()

    def project_step(d, carry):
        project(d)
        return carry

    lax.fori_loop(1, KS + 1, project_step, 0)

    span = (KS + 1) * T
    first = seq * T
    query_where = first + lax.broadcasted_iota(jnp.int32, (T, 1), 0)
    col = lax.broadcasted_iota(jnp.int32, (1, span), 1)
    key_where = first + lax.rem(col, T) - lax.div(col, T) * T
    query_doc = jnp.zeros((T, 1), jnp.int32)
    key_doc = jnp.zeros((1, span), jnp.int32)
    start = jnp.int32(0)
    for n in range(lengths.shape[1]):
        query_doc += (query_where >= start).astype(jnp.int32)
        key_doc += (key_where >= start).astype(jnp.int32)
        start = start + lengths[0, n]
    allowed = (query_doc == key_doc) & (key_where <= query_where) & (key_where >= 0)
    bias = jnp.where(allowed, 0.0, -1e30)
    scale = 1.0 / math.sqrt(NOPE + ROPE)
    half = lax.broadcasted_iota(jnp.int32, (T, 2 * ROPE), 1) < ROPE

    def head_pair(pair, carry):
        pair_lanes = pl.ds(pl.multiple_of(pair * 128, 128), 128)
        q_pair = query_rope[0, :, pair_lanes]
        for odd in range(2):
            lanes = pl.ds(pl.multiple_of((pair * 2 + odd) * NOPE, 128), NOPE)
            q_two = jnp.where(half, q_pair, 0.0) if odd == 0 else jnp.where(half, 0.0, q_pair)
            q = jnp.concatenate([query_nope[0, :, lanes], q_two.astype(BF16)], axis=1)
            rope_keys = latents[:, :, LATENT:].reshape(span, 2 * ROPE)
            k = jnp.concatenate([keys[:, lanes], rope_keys], axis=1)
            scores = dot_t(q, k) * scale + bias
            weights = jnp.exp(scores - jnp.max(scores, axis=1, keepdims=True))
            totals = jnp.sum(weights, axis=1, keepdims=True)
            mixed = dot(weights.astype(BF16), values[:, lanes])
            head_out[:, lanes] = (mixed / totals).astype(BF16)
        return carry

    lax.fori_loop(0, HEADS // 2, head_pair, 0)

    loads[2].wait()

    def project_out(i, squares):
        lanes = pl.ds(pl.multiple_of(i * 512, 512), 512)
        rows = residual[0, :, lanes].astype(F32) + dot(head_out[...], proj[:, lanes])
        hidden[:, lanes] = rows
        return squares + jnp.sum(rows * rows, axis=1, keepdims=True)

    squares = lax.fori_loop(0, D // 512, project_out, jnp.zeros((T, 1), F32))
    inverse = lax.rsqrt(squares * (1.0 / D) + 1e-06)
    normed = (hidden[...] * inverse * gain[...].astype(F32)).astype(BF16)
    tok[0, :, EXTRA:] = normed
    chances = jax.nn.sigmoid(dot(normed, router[...]))
    chosen = [jnp.sum(hit * chances, axis=1, keepdims=True) for hit in hits]
    norm_by = 2.446 / functools.reduce(jnp.add, chosen)
    lane = iota((T, EXTRA), 1)
    extra = jnp.zeros((T, EXTRA), F32)
    for j in range(TOP):
        extra = jnp.where(lane == j, id_cols[:, j : j + 1], extra)
        extra = jnp.where(lane == 8 + j, ranks[j], extra)
        extra = jnp.where(lane == 16 + j, chosen[j] * norm_by, extra)
    tok[0, :, :EXTRA] = extra.astype(BF16)

    ring = {}

    def ring_send(c, hop):
        for way, dz in ((0, 1), (1, -1)):
            if hop == NZ // 2 and c % 2 != way:
                continue
            src = (hop - 1) if way == 0 else (NZ - hop + 1) % NZ
            dst = hop if way == 0 else NZ - hop
            lanes = lanes_of(c)
            copy = send(
                tok.at[src, :, lanes],
                tok.at[dst, :, lanes],
                z_send.at[way, hop - 1, c],
                z_recv.at[way, hop - 1, c],
                peer(dz=dz),
            )
            ring[c, hop, way] = copy
            started.append(copy)

    def ring_wait(c, hop):
        for way in range(2):
            if (c, hop, way) in ring:
                ring[c, hop, way].wait_recv()

    def build(s):
        x = tok[s, :, :EXTRA].astype(F32)
        source = (s * 1024).astype(F32)
        x_t = x.T
        rows = code_rows[...]
        match = None
        for j in range(TOP):
            code = x_t[j : j + 1, :] * 16.0 + x_t[8 + j : 9 + j, :] + source
            hit = rows == code
            match = hit if match is None else match | hit
        lanes = pl.ds(pl.multiple_of(s * T, T), T)
        pick[:, lanes] = match.astype(F32).astype(BF16)
        cols = code_cols[0:1, :]
        weight = jnp.zeros((T, WORK), F32)
        for j in range(TOP):
            code = x[:, j : j + 1] * 16.0 + x[:, 8 + j : 9 + j] + source
            weight = jnp.where(cols == code, x[:, 16 + j : 17 + j], weight)
        put[lanes, :] = weight.astype(BF16)

    def build_two(first_s, step, count):
        def body(i, carry):
            build(first_s + i * step)
            return carry

        lax.fori_loop(0, count, body, 0)

    handed = {}

    def hand_out(c):
        lanes = pl.ds(c * CW, CW)
        tok_lanes = pl.ds(EXTRA + c * CW, CW)

        def body(i, carry):
            rows = pl.ds(pl.multiple_of(i * (WORK // 2), WORK // 2), WORK // 2)
            block = tok[:, :, tok_lanes].reshape(NZ * T, CW)
            outbox[rows, lanes] = dot(pick[rows, :], block).astype(BF16)
            return carry

        lax.fori_loop(0, 2, body, 0)
        for b in range(1, 2 * NY):
            rows = pl.ds(b * BLOCK, BLOCK)
            copy = send(
                outbox.at[rows, lanes],
                work.at[rows, lanes],
                y_send.at[b, c],
                y_recv.at[b, c],
                peer(dy=b // 2, dc=b % 2),
            )
            handed[c, b] = copy
            started.append(copy)
        work[:BLOCK, lanes] = outbox[:BLOCK, lanes]

    far = []

    def weights_onward():
        for copy in near:
            copy.wait_recv()
        for way, (ref, dx) in enumerate(((w_gate, 1), (w_up, -1))):
            copy = send(
                ref.at[1 + way], ref.at[3], f_send.at[way], f_recv.at[way], peer(dx=dx)
            )
            far.append(copy)
            started.append(copy)
        for j in range(NJ):
            lanes = pl.ds(j * JW, JW)
            for way, dx in ((0, 1), (1, -1)):
                copy = send(
                    down_in.at[0, 0, :, lanes],
                    w_down.at[1 + way, :, lanes],
                    d_send.at[way, j],
                    d_recv.at[way, j],
                    peer(dx=dx),
                )
                down_near[j, way] = copy
                started.append(copy)

    down_near = {}
    down_far = {}

    def down_onward(j):
        lanes = pl.ds(j * JW, JW)
        for way in range(2):
            down_near[j, way].wait_recv()
        way, dx = (0, 1) if j % 2 == 0 else (1, -1)
        copy = send(
            w_down.at[1 + way, :, lanes],
            w_down.at[3, :, lanes],
            e_send.at[j],
            e_recv.at[j],
            peer(dx=dx),
        )
        down_far[j] = copy
        started.append(copy)

    ring_send(0, 1)
    ring_send(1, 1)
    build_two(0, 1, 1)
    events = sorted((2 * c + hop, c, hop) for c in range(NC) for hop in range(1, NZ // 2 + 1))
    for _, c, hop in events:
        ring_wait(c, hop)
        if hop < NZ // 2:
            ring_send(c, hop + 1)
        if hop == 2 and c + 2 < NC:
            ring_send(c + 2, 1)
        if c == 0:
            if hop < NZ // 2:
                build_two(hop, NZ - 2 * hop, 2)
            else:
                build_two(hop, 1, 1)
        if hop == NZ // 2:
            hand_out(c)
            if c == NC - 2:
                weights_onward()
    for c in range(NC):
        for b in range(1, 2 * NY):
            handed[c, b].wait_recv()

    for copy in loads[3:]:
        copy.wait()
    tile = 256

    def hidden_units(w):
        def body(i, carry):
            rows = pl.ds(pl.multiple_of(i * tile, tile), tile)
            x = work[rows, :]
            g = dot(x, w_gate[w])
            units[w, rows, :] = (g * jax.nn.sigmoid(g) * dot(x, w_up[w])).astype(BF16)
            return carry

        lax.fori_loop(0, WORK // tile, body, 0)

    for w in range(4):
        if w == 3:
            for copy in far:
                copy.wait_recv()
            down_onward(0)
        hidden_units(w)

    for copy in handed.values():
        copy.wait_send()
    back = {}

    def answer(j):
        lanes = pl.ds(j * JW, JW)
        down_far[j].wait_recv()

        def body(i, carry):
            rows = pl.ds(pl.multiple_of(i * tile, tile), tile)
            total = dot(units[0, rows, :], w_down[0, :, lanes])
            for w in range(1, 4):
                total += dot(units[w, rows, :], w_down[w, :, lanes])
            outbox[rows, lanes] = total.astype(BF16)
            return carry

        lax.fori_loop(0, WORK // tile, body, 0)
        for b in range(1, 2 * NY):
            rows = pl.ds(b * BLOCK, BLOCK)
            copy = send(
                outbox.at[rows, lanes],
                inbox.at[rows, lanes],
                r_send.at[b, j],
                r_recv.at[b, j],
                peer(dy=-(b // 2), dc=b % 2),
            )
            back[j, b] = copy
            started.append(copy)
        inbox[:BLOCK, lanes] = outbox[:BLOCK, lanes]

    sums = {}

    def sum_send(j, way, left):
        lanes = pl.ds(j * JW, JW)
        slot = left if way == 0 else NZ - left
        where = NZ // 2 * 2 - 2 if left == NZ // 2 else way * (NZ // 2 - 1) + left - 1
        copy = send(
            zs.at[slot, :, lanes],
            zr.at[where, :, lanes],
            s_send.at[way, left - 1, j],
            s_recv.at[way, left - 1, j],
            peer(dz=-1 if way == 0 else 1),
        )
        sums[j, way, left] = (copy, where)
        started.append(copy)

    def combine(j):
        lanes = pl.ds(j * JW, JW)
        for b in range(1, 2 * NY):
            back[j, b].wait_recv()

        def body(i, carry):
            rows = pl.ds(pl.multiple_of(i * 2 * T, 2 * T), 2 * T)
            total = dot(put[rows, :], inbox[:, lanes]).astype(BF16)
            zs[2 * i, :, lanes] = total[:T]
            zs[2 * i + 1, :, lanes] = total[T:]
            return carry

        lax.fori_loop(0, NZ // 2, body, 0)
        long_way = j % 2
        sum_send(j, long_way, NZ // 2)
        sum_send(j, 1 - long_way, NZ // 2 - 1)

    def reduce_step(j, hop):
        lanes = pl.ds(j * JW, JW)
        long_way = j % 2
        for way, left in ((long_way, NZ // 2 + 1 - hop), (1 - long_way, NZ // 2 - hop)):
            if left < 1:
                continue
            copy, where = sums[j, way, left]
            copy.wait_recv()
            if left > 1:
                slot = left - 1 if way == 0 else NZ - left + 1
                total = zs[slot, :, lanes].astype(F32) + zr[where, :, lanes].astype(F32)
                zs[slot, :, lanes] = total.astype(BF16)
                sum_send(j, way, left - 1)
        if hop == NZ // 2:
            total = hidden[:, lanes] + zs[0, :, lanes].astype(F32)
            for way in range(2):
                total += zr[sums[j, way, 1][1], :, lanes].astype(F32)
            out[0, :, lanes] = total.astype(BF16)

    steps = []
    for j in range(NJ):
        steps.append((3 * j, 0, j, "answer"))
        steps.append((3 * j + 3.5, 0, j, "combine"))
        for hop in range(1, NZ // 2 + 1):
            steps.append((3 * j + 4.5 + 1.1 * hop, 1, j, hop))
    for _, _, j, what in sorted(steps, key=lambda step: step[:3]):
        if what == "answer":
            if j + 1 < NJ:
                down_onward(j + 1)
            answer(j)
        elif what == "combine":
            combine(j)
        else:
            reduce_step(j, what)

    for copy in started:
        if not any(copy is other for other in handed.values()):
            copy.wait_send()


def on_device(
    residual,
    query_nope,
    query_rope,
    latent_rows,
    key_rope,
    key_up,
    value_up,
    output_proj,
    doc_lengths,
    norm_gain,
    router_weight,
    expert_ids,
    gate_quarter,
    up_quarter,
    down_quarter,
):
    vmem = pl.BlockSpec(memory_space=pltpu.VMEM)
    smem = pl.BlockSpec(memory_space=pltpu.SMEM)
    anywhere = pl.BlockSpec(memory_space=pl.ANY)
    dma = pltpu.SemaphoreType.DMA
    hops = NZ // 2
    span = (KS + 1) * T
    return pl.pallas_call(
        kernel,
        out_shape=jax.ShapeDtypeStruct((1, T, D), BF16),
        in_specs=[vmem] * 5 + [smem] + [vmem] * 3 + [anywhere] * 6,
        out_specs=vmem,
        scratch_shapes=[
            pltpu.VMEM((LATENT, HEADS * NOPE), BF16),
            pltpu.VMEM((LATENT, HEADS * NOPE), BF16),
            pltpu.VMEM((HEADS * NOPE, D), BF16),
            pltpu.VMEM((4, D, FQ), BF16),
            pltpu.VMEM((4, D, FQ), BF16),
            pltpu.VMEM((4, FQ, D), BF16),
            pltpu.VMEM((KS + 1, T, LATENT + 2 * ROPE), BF16),
            pltpu.VMEM((span, HEADS * NOPE), BF16),
            pltpu.VMEM((span, HEADS * NOPE), BF16),
            pltpu.VMEM((T, HEADS * NOPE), BF16),
            pltpu.VMEM((T, D), F32),
            pltpu.VMEM((NZ, T, EXTRA + D), BF16),
            pltpu.VMEM((WORK, T), F32),
            pltpu.VMEM((8, WORK), F32),
            pltpu.VMEM((WORK, NZ * T), BF16),
            pltpu.VMEM((NZ * T, WORK), BF16),
            pltpu.VMEM((WORK, D), BF16),
            pltpu.VMEM((WORK, D), BF16),
            pltpu.VMEM((4, WORK, FQ), BF16),
            pltpu.VMEM((WORK, D), BF16),
            pltpu.VMEM((NZ, T, D), BF16),
            pltpu.VMEM((NZ - 1, T, D), BF16),
            dma((6,)),
            dma((KS,)),
            dma((KS,)),
            dma((2, 2)),
            dma((2, 2)),
            dma((2,)),
            dma((2,)),
            dma((2, NJ)),
            dma((2, NJ)),
            dma((NJ,)),
            dma((NJ,)),
            dma((2, hops, NC)),
            dma((2, hops, NC)),
            dma((2 * NY, NC)),
            dma((2 * NY, NC)),
            dma((2 * NY, NJ)),
            dma((2 * NY, NJ)),
            dma((2, hops, NJ)),
            dma((2, hops, NJ)),
        ],
        compiler_params=pltpu.CompilerParams(
            collective_id=0, has_side_effects=True, vmem_limit_bytes=62 * 2**20
        ),
        cost_estimate=pl.CostEstimate(
            flops=24 * 10**9, bytes_accessed=30 * 10**6, transcendentals=10**6
        ),
        name="layer",
    )(
        residual,
        query_nope,
        query_rope,
        latent_rows,
        key_rope,
        doc_lengths,
        norm_gain.reshape(1, D),
        router_weight,
        expert_ids,
        key_up,
        value_up,
        output_proj,
        gate_quarter,
        up_quarter,
        down_quarter,
    )


def solution(mesh):
    in_specs = (
        P("exp", "seq", None),
        P("exp", "seq", None),
        P("exp", "seq", None),
        P("exp", "seq", None),
        P("exp", "seq", None),
        P(),
        P(),
        P(),
        P("exp", None),
        P(),
        P(),
        P("exp", "seq", None),
        P("seq", "exp", None, None),
        P("seq", "exp", None, None),
        P("seq", "exp", None, None),
    )
    return jax.shard_map(
        on_device, mesh=mesh, in_specs=in_specs, out_specs=P("exp", "seq", None), check_vma=False
    )
```

time: 655 us -> 254 us (0.39); the launches traced: 645 us -> 253 us
  waiting for transfers between devices: 312 us -> 0 us
  Pallas kernels: 0 us -> 240 us
  local copies, waits for them, and re-layouts: 109 us -> 12.2 us
  blocking collectives: 77 us -> 0 us
  matrix products: 67.6 us -> 0 us
  starting transfers between devices: 53.5 us -> 0 us
  other arithmetic: 24.5 us -> 0 us
    ppermute x15 -> x0, waiting for transfers between devices: 249 us -> none  [the longest x6 230 us: partner_2(): return lax.ppermute(value, axis, pairs)]
    pallas_call x0 -> x1, Pallas kernels: none -> 240 us  [on_device(): pl.pallas_call(kernel, out_shape=jax.ShapeDtypeStruct((1, T, D), BF16), i...]
    all_to_all x2 -> x0, blocking collectives: 77 us -> none  [the longest x1 41.6 us: on_device(): lax.all_to_all(answered, 'seq', split_axis=0, concat_axis=0, tiled=True)]
    dot_general x24 -> x0, matrix products: 67.6 us -> none  [the longest x4 39.1 us: on_device(): jnp.dot(activation.astype(jnp.bfloat16), quarters[2][member_index], prefe...]
    all_to_all x2 -> x0, waiting for transfers between devices: 63.1 us -> none  [the longest x1 63.1 us: on_device(): lax.all_to_all(lax.all_to_all(answered, 'seq', split_axis=0, concat_axis=...]
    reshape x10 -> x1, local copies, waits for them, and re-layouts: 42.1 us -> 1.29 us  [on_device(): norm_gain.reshape(1, D)]
    ppermute x15 -> x0, starting transfers between devices: 37.5 us -> none  [the longest x9 28.8 us: passed_along(): return lax.ppermute(block, axis, route)]
    scatter x1 -> x0, local copies, waits for them, and re-layouts: 29 us -> none  [on_device(): outgoing = jnp.zeros((seq_count * exp_count * slot_count, D), jnp.bfloat1...]
  transfers between devices with their start and end apart: 17 -> 0, of which waited for: 8 -> 0; matrix products, arithmetic and copies ran while one was open for 13% -> 0% of each run, Pallas kernels for 0% -> 0%
where the time goes in v1:
time: 254 us; the launch traced here: 253 us
  Pallas kernels  240 us (94%)
  local copies, waits for them, and re-layouts  12.2 us (5%)
    pallas_call x1, Pallas kernels, on_device(): pl.pallas_call(kernel, out_shape=jax.ShapeDtypeStruct((1, T, D), BF16), i...  240 us
    unnamed x8, local copies, waits for them, and re-layouts  10.9 us

profile of v1, /device:TPU:8, one launch (start us, length us, event | category | flops | bytes accessed | tf_op | source)
XLA Modules:
  0.0 252.7 jit_solution(14623555806655931830)
XLA Ops:
  0.0 1.3 reshape.3.gain
  1.3 1.4 copy.16.rope
  2.7 1.4 copy.18.ids
  4.1 2.0 copy.17.router
  6.1 0.0 copy-start
  6.1 2.7 %copy.19.gate_in = bf16[1,1,2048,352]{3,2,1,0:T(8,128)(2,1)} copy(bf16[1,1,2048,352]{2,3,1,0:T(8,128)(2,1)} %param.27) | data formatting | bytes 2883584 | tf_op args[12]
  8.8 0.0 copy-done
  8.8 1.6 copy.20.up_in
  10.3 240.5 %layer.1 = bf16[1,128,2048]{2,1,0:T(8,128)(2,1)} custom-call(bf16[1,128,2048]{2,1,0:T(8,128)(2,1)} %residual.1, bf16[1,128,1024]{2,1,0:T(8,128)(2,1)} %query_nope.1, bf16[1,128,512]{2,1,0:T(8,128)(2,1)} %query_rope.1, bf16[1,128,512]{2,1,0:T(8,128)(2,1)} %latent.1, bf16[1,128,64]{2,1,0:T(8,128)(2,1)} %copy.16.rope, s32[1,8]{1,0:T(1,128)} %lengths.1, ...), custom_call_target="tpu_custom_call" | custom-call | flops 24000000000 | bytes 30000000 | tf_op jit(solution)/shard_map/layer/pallas_call | solution.py:581
  250.8 1.9 copy.22
Async XLA Ops:
  6.1 2.7 %copy-start = (bf16[1,1,2048,352]{2,3,1,0:T(8,128)(2,1)S(1)}, bf16[1,1,2048,352]{2,3,1,0:T(8,128)(2,1)}, u32[]{:S(2)}) copy-start(bf16[1,1,2048,352]{2,3,1,0:T(8,128)(2,1)} %param.28) | copy-start | bytes 4325380

commit v2 on v1

--- a/solution.py
+++ b/solution.py
@@ -29,7 +29,12 @@
 EXTRA = 128
 NC = 4
 CW = D // NC
-NJ = 4
+LATE = 0
+AHEAD = 3
+PACE = 1
+PLAN = {("hop", 6): [("near", 0)], ("hop", 8): [("near", 1)], ("hop", 10): [("on", 0)], ("hop", 13): [("near", 2)], ("hop", 15): [("near", 3)], ("quarter", 1): [("far", 0), ("near", 4)], ("quarter", 2): [("far", 1), ("near", 5)], ("quarter", 3): [("far", 2), ("near", 6)], ("answer", 0): [("far", 3), ("near", 7)], ("answer", 1): [("far", 4)], ("answer", 2): [("far", 5)], ("answer", 3): [("far", 6)], ("answer", 4): [("far", 7)]}
+HOP_START, HOP_PACE = 3.5, 3.0
+NJ = 8
 JW = D // NJ
 
 
@@ -39,6 +44,10 @@
 
 def dot_t(a, b):
     return lax.dot_general(a, b, (((1,), (1,)), ((), ())), preferred_element_type=F32)
+
+
+def t_dot(a, b):
+    return lax.dot_general(a, b, (((0,), (0,)), ((), ())), preferred_element_type=F32)
 
 
 def iota(shape, dim):
@@ -166,7 +175,7 @@
         == lax.broadcasted_iota(jnp.int32, (ROPE, 2 * ROPE), 0)
     ).astype(F32).astype(BF16)
     latents[0, :, :LATENT] = latent[0]
-    latents[0, :, LATENT:] = dot(rope[0], twice).astype(BF16)
+    latents[0, :, LATENT:] = t_dot(rope[0], twice).astype(BF16)
 
     pl.semaphore_wait(barrier, len(partners))
 
@@ -177,16 +186,36 @@
         started.append(copy)
 
     near = []
-    for i, (src, dst) in enumerate(((gate_in, w_gate), (up_in, w_up))):
+    down_near = {}
+
+    def weights_near():
+        for i, (src, dst) in enumerate(((gate_in, w_gate), (up_in, w_up))):
+            for way, dx in ((0, 1), (1, -1)):
+                copy = send(
+                    src.at[0, 0], dst.at[1 + way], w_send.at[i, way], w_recv.at[i, way], peer(dx=dx)
+                )
+                near.append(copy)
+                started.append(copy)
+
+    def down_to_neighbours(j):
+        lanes = pl.ds(j * JW, JW)
         for way, dx in ((0, 1), (1, -1)):
             copy = send(
-                src.at[0, 0], dst.at[1 + way], w_send.at[i, way], w_recv.at[i, way], peer(dx=dx)
+                down_in.at[0, 0, :, lanes],
+                w_down.at[1 + way, :, lanes],
+                d_send.at[way, j],
+                d_recv.at[way, j],
+                peer(dx=dx),
             )
-            near.append(copy)
+            down_near[j, way] = copy
             started.append(copy)
 
+    if not LATE:
+        weights_near()
+
     lane_e = iota((T, EXPERTS), 1)
-    id_cols = ids[0].astype(F32)
+    id_rows = jnp.concatenate([ids[j].astype(F32) for j in range(TOP)] + [jnp.zeros((2, T), F32)], 0)
+    id_cols = id_rows.T
     hits = [(id_cols[:, j : j + 1] == lane_e).astype(F32) for j in range(TOP)]
     named = functools.reduce(jnp.add, hits)
     lower = (
@@ -225,6 +254,8 @@
     project(0)
     for copy in arriving:
         copy.wait_recv()
+    if LATE:
+        weights_near()
 
     def project_step(d, carry):
         project(d)
@@ -277,9 +308,9 @@
 
     squares = lax.fori_loop(0, D // 512, project_out, jnp.zeros((T, 1), F32))
     inverse = lax.rsqrt(squares * (1.0 / D) + 1e-06)
-    normed = (hidden[...] * inverse * gain[...].astype(F32)).astype(BF16)
+    normed = (hidden[...] * inverse * gain[...].astype(F32).reshape(1, D)).astype(BF16)
     tok[0, :, EXTRA:] = normed
-    chances = jax.nn.sigmoid(dot(normed, router[...]))
+    chances = jax.nn.sigmoid(dot_t(normed, router[...]))
     chosen = [jnp.sum(hit * chances, axis=1, keepdims=True) for hit in hits]
     norm_by = 2.446 / functools.reduce(jnp.add, chosen)
     lane = iota((T, EXTRA), 1)
@@ -377,20 +408,7 @@
             )
             far.append(copy)
             started.append(copy)
-        for j in range(NJ):
-            lanes = pl.ds(j * JW, JW)
-            for way, dx in ((0, 1), (1, -1)):
-                copy = send(
-                    down_in.at[0, 0, :, lanes],
-                    w_down.at[1 + way, :, lanes],
-                    d_send.at[way, j],
-                    d_recv.at[way, j],
-                    peer(dx=dx),
-                )
-                down_near[j, way] = copy
-                started.append(copy)
-
-    down_near = {}
+
     down_far = {}
 
     def down_onward(j):
@@ -408,16 +426,25 @@
         down_far[j] = copy
         started.append(copy)
 
-    ring_send(0, 1)
-    ring_send(1, 1)
+    def feed(*place):
+        for what, j in PLAN.get(place, ()):
+            if what == "on":
+                weights_onward()
+            elif what == "near":
+                down_to_neighbours(j)
+            else:
+                down_onward(j)
+
+    for c in range(AHEAD):
+        ring_send(c, 1)
     build_two(0, 1, 1)
-    events = sorted((2 * c + hop, c, hop) for c in range(NC) for hop in range(1, NZ // 2 + 1))
-    for _, c, hop in events:
+    events = sorted((PACE * c + hop, c, hop) for c in range(NC) for hop in range(1, NZ // 2 + 1))
+    for index, (_, c, hop) in enumerate(events):
         ring_wait(c, hop)
         if hop < NZ // 2:
             ring_send(c, hop + 1)
-        if hop == 2 and c + 2 < NC:
-            ring_send(c + 2, 1)
+        if hop == 1 and c + AHEAD < NC:
+            ring_send(c + AHEAD, 1)
         if c == 0:
             if hop < NZ // 2:
                 build_two(hop, NZ - 2 * hop, 2)
@@ -425,8 +452,7 @@
                 build_two(hop, 1, 1)
         if hop == NZ // 2:
             hand_out(c)
-            if c == NC - 2:
-                weights_onward()
+        feed("hop", index)
     for c in range(NC):
         for b in range(1, 2 * NY):
             handed[c, b].wait_recv()
@@ -439,8 +465,8 @@
         def body(i, carry):
             rows = pl.ds(pl.multiple_of(i * tile, tile), tile)
             x = work[rows, :]
-            g = dot(x, w_gate[w])
-            units[w, rows, :] = (g * jax.nn.sigmoid(g) * dot(x, w_up[w])).astype(BF16)
+            g = dot_t(x, w_gate[w])
+            units[w, rows, :] = (g * jax.nn.sigmoid(g) * dot_t(x, w_up[w])).astype(BF16)
             return carry
 
         lax.fori_loop(0, WORK // tile, body, 0)
@@ -449,8 +475,8 @@
         if w == 3:
             for copy in far:
                 copy.wait_recv()
-            down_onward(0)
         hidden_units(w)
+        feed("quarter", w)
 
     for copy in handed.values():
         copy.wait_send()
@@ -539,12 +565,11 @@
         steps.append((3 * j, 0, j, "answer"))
         steps.append((3 * j + 3.5, 0, j, "combine"))
         for hop in range(1, NZ // 2 + 1):
-            steps.append((3 * j + 4.5 + 1.1 * hop, 1, j, hop))
+            steps.append((3 * j + HOP_START + HOP_PACE * hop, 1, j, hop))
     for _, _, j, what in sorted(steps, key=lambda step: step[:3]):
         if what == "answer":
-            if j + 1 < NJ:
-                down_onward(j + 1)
             answer(j)
+            feed("answer", j)
         elif what == "combine":
             combine(j)
         else:
@@ -587,8 +612,8 @@
             pltpu.VMEM((LATENT, HEADS * NOPE), BF16),
             pltpu.VMEM((LATENT, HEADS * NOPE), BF16),
             pltpu.VMEM((HEADS * NOPE, D), BF16),
-            pltpu.VMEM((4, D, FQ), BF16),
-            pltpu.VMEM((4, D, FQ), BF16),
+            pltpu.VMEM((4, FQ, D), BF16),
+            pltpu.VMEM((4, FQ, D), BF16),
             pltpu.VMEM((4, FQ, D), BF16),
             pltpu.VMEM((KS + 1, T, LATENT + 2 * ROPE), BF16),
             pltpu.VMEM((span, HEADS * NOPE), BF16),
@@ -638,16 +663,16 @@
         query_nope,
         query_rope,
         latent_rows,
-        key_rope,
+        key_rope.transpose(0, 2, 1),
         doc_lengths,
-        norm_gain.reshape(1, D),
-        router_weight,
-        expert_ids,
+        norm_gain,
+        router_weight.T,
+        expert_ids.transpose(2, 0, 1),
         key_up,
         value_up,
         output_proj,
-        gate_quarter,
-        up_quarter,
+        gate_quarter.transpose(0, 1, 3, 2),
+        up_quarter.transpose(0, 1, 3, 2),
         down_quarter,
     )
 

time: 254 us -> 208 us (0.82)
  Pallas kernels: 240 us -> 206 us
  local copies, waits for them, and re-layouts: 12.2 us -> 1.88 us
    pallas_call x1, Pallas kernels: 240 us -> 206 us  [on_device(): pl.pallas_call(kernel, out_shape=jax.ShapeDtypeStruct((1, T, D), BF16), i...]
    unnamed x8 -> x1, local copies, waits for them, and re-layouts: 10.9 us -> 1.88 us
where the time goes in v2:
time: 208 us
  Pallas kernels  206 us (99%)
    pallas_call x1, Pallas kernels, on_device(): pl.pallas_call(kernel, out_shape=jax.ShapeDtypeStruct((1, T, D), BF16), i...  206 us

profile of v2, /device:TPU:8, one launch (start us, length us, event | category | flops | bytes accessed | tf_op | source)
XLA Modules:
  0.0 207.7 jit_solution(12146726686237783964)
XLA Ops:
  0.0 205.9 %layer.1 = bf16[1,128,2048]{2,1,0:T(8,128)(2,1)} custom-call(bf16[1,128,2048]{2,1,0:T(8,128)(2,1)} %residual.1, bf16[1,128,1024]{2,1,0:T(8,128)(2,1)} %query_nope.1, bf16[1,128,512]{2,1,0:T(8,128)(2,1)} %query_rope.1, bf16[1,128,512]{2,1,0:T(8,128)(2,1)} %latent.1, bf16[1,64,128]{2,1,0:T(8,128)(2,1)} %bitcast.8, s32[1,8]{1,0:T(1,128)} %lengths.1, ...), custom_call_target="tpu_custom_call" | custom-call | flops 24000000000 | bytes 30000000 | tf_op jit(solution)/shard_map/layer/pallas_call | solution.py:606
  205.9 1.9 copy.17

commit v3 on v2

--- a/solution.py
+++ b/solution.py
@@ -29,7 +29,7 @@
 EXTRA = 128
 NC = 4
 CW = D // NC
-LATE = 0
+LATE = 1
 AHEAD = 3
 PACE = 1
 PLAN = {("hop", 6): [("near", 0)], ("hop", 8): [("near", 1)], ("hop", 10): [("on", 0)], ("hop", 13): [("near", 2)], ("hop", 15): [("near", 3)], ("quarter", 1): [("far", 0), ("near", 4)], ("quarter", 2): [("far", 1), ("near", 5)], ("quarter", 3): [("far", 2), ("near", 6)], ("answer", 0): [("far", 3), ("near", 7)], ("answer", 1): [("far", 4)], ("answer", 2): [("far", 5)], ("answer", 3): [("far", 6)], ("answer", 4): [("far", 7)]}
@@ -188,14 +188,14 @@
     near = []
     down_near = {}
 
-    def weights_near():
-        for i, (src, dst) in enumerate(((gate_in, w_gate), (up_in, w_up))):
-            for way, dx in ((0, 1), (1, -1)):
-                copy = send(
-                    src.at[0, 0], dst.at[1 + way], w_send.at[i, way], w_recv.at[i, way], peer(dx=dx)
-                )
-                near.append(copy)
-                started.append(copy)
+    def weights_near(i):
+        src, dst = ((gate_in, w_gate), (up_in, w_up))[i]
+        for way, dx in ((0, 1), (1, -1)):
+            copy = send(
+                src.at[0, 0], dst.at[1 + way], w_send.at[i, way], w_recv.at[i, way], peer(dx=dx)
+            )
+            near.append(copy)
+            started.append(copy)
 
     def down_to_neighbours(j):
         lanes = pl.ds(j * JW, JW)
@@ -210,8 +210,8 @@
             down_near[j, way] = copy
             started.append(copy)
 
-    if not LATE:
-        weights_near()
+    for i in range(2 - LATE):
+        weights_near(i)
 
     lane_e = iota((T, EXPERTS), 1)
     id_rows = jnp.concatenate([ids[j].astype(F32) for j in range(TOP)] + [jnp.zeros((2, T), F32)], 0)
@@ -252,17 +252,6 @@
         values[rows, :] = dot(block, value_up[...]).astype(BF16)
 
     project(0)
-    for copy in arriving:
-        copy.wait_recv()
-    if LATE:
-        weights_near()
-
-    def project_step(d, carry):
-        project(d)
-        return carry
-
-    lax.fori_loop(1, KS + 1, project_step, 0)
-
     span = (KS + 1) * T
     first = seq * T
     query_where = first + lax.broadcasted_iota(jnp.int32, (T, 1), 0)
@@ -278,6 +267,11 @@
     allowed = (query_doc == key_doc) & (key_where <= query_where) & (key_where >= 0)
     bias = jnp.where(allowed, 0.0, -1e30)
     scale = 1.0 / math.sqrt(NOPE + ROPE)
+    for d, copy in enumerate(arriving):
+        copy.wait_recv()
+        project(d + 1)
+    for i in range(2 - LATE, 2):
+        weights_near(i)
     half = lax.broadcasted_iota(jnp.int32, (T, 2 * ROPE), 1) < ROPE
 
     def head_pair(pair, carry):

time: 208 us -> 208 us (level)
  no operation moved by 1% of the time
where the time goes in v3:
time: 208 us
  Pallas kernels  206 us (99%)
    pallas_call x1, Pallas kernels, on_device(): pl.pallas_call(kernel, out_shape=jax.ShapeDtypeStruct((1, T, D), BF16), i...  206 us

profile of v3, /device:TPU:8, one launch (start us, length us, event | category | flops | bytes accessed | tf_op | source)
XLA Modules:
  0.0 207.7 jit_solution(13408886189928725982)
XLA Ops:
  0.0 205.9 %layer.1 = bf16[1,128,2048]{2,1,0:T(8,128)(2,1)} custom-call(bf16[1,128,2048]{2,1,0:T(8,128)(2,1)} %residual.1, bf16[1,128,1024]{2,1,0:T(8,128)(2,1)} %query_nope.1, bf16[1,128,512]{2,1,0:T(8,128)(2,1)} %query_rope.1, bf16[1,128,512]{2,1,0:T(8,128)(2,1)} %latent.1, bf16[1,64,128]{2,1,0:T(8,128)(2,1)} %bitcast.8, s32[1,8]{1,0:T(1,128)} %lengths.1, ...), custom_call_target="tpu_custom_call" | custom-call | flops 24000000000 | bytes 30000000 | tf_op jit(solution)/shard_map/layer/pallas_call | solution.py:600
  205.9 1.9 copy.17
